TPU v7x, 32 devices: a whole 2x2x4 slice. The times are simulated.
32 devices in a mesh: subj: 8 (over z, y), vox: 4 (over x, core).
Axes of the slice: x: 2, y: 2, z: 4, core: 2. Of those that a mesh axis runs over, the one named last changes fastest.
Arguments:
- scans: bfloat16 [5120, 49152], P('subj', 'vox'), may hold values from -6 to 6
- test_matrix: bfloat16 [49152, 128], P('vox'), may hold values from -6 to 6
- lengths: int32 [8], replicated, may hold values from 160 to 640, as said below
- block_subject: int32 [8], replicated, may hold values from 0 to 7, each once
Outputs:
- basis: float32 [49152, 128], P('vox')
Inputs may be any that keep to these rules, and one draw needn't show every extreme that they name: `lengths`: one subject has exactly 640 rows and one exactly 160. `block_subject`: each subject appears once.
All inputs are finite; a program needn't handle non-finite values.
Results may differ from a plain program's by a relative error of at most 0.0046.
Values may be sent and summed in bfloat16 or wider, within the bound.
No kernel may reach another device: no remote copies, remote signals or barrier semaphores. Data moves between devices by JAX's collectives and lax.ppermute only.
A program may use at most 128 MiB of HBM per device.

v0:
```python
import jax
import jax.numpy as jnp
from jax import lax
from jax.sharding import PartitionSpec as P

V = 49152
PASSES = 2


def on_device(scans, test_matrix, lengths, block_subject):
    time_rows, voxel_cols = scans.shape
    rank_cols = test_matrix.shape[1]
    position = lax.axis_index("subj")
    slot_ids = jnp.arange(block_subject.shape[0], dtype=jnp.int32)
    subject = jnp.sum(jnp.where(slot_ids == position, block_subject, 0))
    length = jnp.sum(jnp.where(slot_ids == subject, lengths, 0))
    live_rows = (jnp.arange(time_rows, dtype=jnp.int32) < length)[:, None]
    panel_now = test_matrix
    result = jnp.zeros((voxel_cols, rank_cols), jnp.float32)
    for sweep_index in range(PASSES):
        partial_scores = jnp.dot(scans, panel_now, preferred_element_type=jnp.float32)
        summed = lax.psum(partial_scores, "vox")
        scores = jnp.where(live_rows, summed, jnp.float32(0.0)).astype(jnp.bfloat16)
        sketch = lax.psum(
            lax.dot_general(
                scans, scores, (((0,), (0,)), ((), ())), preferred_element_type=jnp.float32
            ),
            "subj",
        )
        local_gram = jnp.dot(sketch.T, sketch, precision=lax.Precision.HIGHEST)
        gram_matrix = lax.psum(local_gram, "vox") / V
        factor = jnp.linalg.cholesky(gram_matrix)
        orthonormal = jax.scipy.linalg.solve_triangular(factor, sketch.T, lower=True).T
        panel_now = orthonormal.astype(jnp.bfloat16)
        result = orthonormal
    return result


def solution(mesh):
    placed = (P("subj", "vox"), P("vox", None), P(), P())
    return jax.shard_map(
        on_device, mesh=mesh, in_specs=placed, out_specs=P("vox", None), check_vma=False
    )
```

profile of v0, /device:TPU:0, one launch (start us, length us, event | category | flops | bytes accessed | tf_op | source)
XLA Modules:
  0.0 661.8 jit_solution(16687764672583974074)
XLA Ops:
  6.5 1.4 fusion.14
  8.0 2.0 fusion.15
  10.7 8.4 %fusion.18 = f32[640,128]{1,0:T(8,128)} fusion(bf16[640,12288]{1,0:T(8,128)(2,1)} %param.7, bf16[12288,128]{1,0:T(8,128)(2,1)S(1)} %copy-done), kind=kOutput, calls=%fused_computation.39 | convolution fusion | flops 2013265920 | bytes 19202048 | tf_op jit(solution)/shard_map/dot_general | solution.py:21
  19.1 17.1 %all-reduce.14 = bf16[640,128]{1,0:T(8,128)(2,1)S(1)} all-reduce(f32[640,128]{1,0:T(8,128)} %fusion.18), channel_id=1, replica_groups=mesh['subj'=8,'vox'=4] {'vox'}, use_global_device_ids=true, to_apply=%region_2.3 | all-reduce | flops 81920 | bytes 491520 | tf_op jit(solution)/shard_map/psum | solution.py:22
  36.2 11.0 %convolution_bitcast_fusion.1 = f32[12288,128]{0,1:T(8,128)} fusion(bf16[640,12288]{1,0:T(8,128)(2,1)} %param.7, bf16[640,128]{1,0:T(8,128)(2,1)S(1)} %all-reduce.14, pred[640]{0:T(1024)(128)(4,1)S(1)} %iota_compare_fusion.2), kind=kOutput, calls=%fused_computation.1 | convolution fusion | flops 2013347840 | bytes 22184576 | tf_op jit(solution)/shard_map/dot_general | solution.py:25
  47.2 212.4 %all-reduce.7.cloned.1.call-done = f32[12288,128]{0,1:T(8,128)} async-done(((f32[12288,128]{0,1:T(8,128)}), f32[12288,128]{0,1:T(8,128)}) %all-reduce.7.cloned.1.call-update) | async-done | bytes 6291472 | tf_op jit(solution)/shard_map/psum | solution.py:24
  259.6 8.8 %fusion.19 = f32[128,128]{0,1:T(8,128)} fusion(f32[12288,128]{0,1:T(8,128)} %all-reduce.7.cloned.1.call-done), kind=kOutput, calls=%fused_computation.40 | convolution fusion | flops 2415919104 | bytes 6356992 | tf_op jit(solution)/shard_map/dot_general | solution.py:30
  268.7 30.0 %all-reduce.9.cloned.1.call-done = f32[128,128]{0,1:T(8,128)} async-done(((f32[128,128]{0,1:T(8,128)}), f32[128,128]{0,1:T(8,128)}) %all-reduce.9.cloned.1.call-update) | async-done | bytes 65552 | tf_op jit(solution)/shard_map/psum | solution.py:31
  298.7 0.8 broadcast_multiply_fusion.1
  299.6 0.9 fusion.11
  300.5 11.7 %cholesky.44 = f32[128,128]{1,0:T(8,128)S(1)} custom-call(f32[128,128]{1,0:T(8,128)S(1)} %fusion.11), custom_call_target="Cholesky" | custom-call | tf_op jit(solution)/shard_map/jit(cholesky)/cholesky | solution.py:32
  313.5 9.8 %custom-call.6 = f32[1,128,128]{1,2,0:T(8,128)S(1)} custom-call(f32[1,128,128]{2,1,0:T(8,128)S(1)} %fusion.6), custom_call_target="InvertDiagBlocksLowerTriangular" | custom-call | tf_op jit(solution)/shard_map/jit(_solve_triangular)/triangular_solve | solution.py:33
  323.3 7.6 %convolution_convert_fusion = bf16[128,12288]{1,0:T(8,128)(2,1)S(1)} fusion(f32[12288,128]{0,1:T(8,128)} %all-reduce.7.cloned.1.call-done, f32[1,128,128]{1,2,0:T(8,128)S(1)} %custom-call.6), kind=kOutput, calls=%fused_computation.3 | convolution fusion | flops 2417491968 | bytes 9502720 | tf_op jit(solution)/shard_map/jit(_solve_triangular)/triangular_solve | solution.py:33
  330.9 7.7 %convolution_bitcast_fusion.3 = f32[640,128]{1,0:T(8,128)S(1)} fusion(bf16[128,12288]{1,0:T(8,128)(2,1)S(1)} %convolution_convert_fusion, bf16[640,12288]{1,0:T(8,128)(2,1)} %param.7), kind=kOutput, calls=%fused_computation.6 | convolution fusion | flops 2013265920 | bytes 19202048 | tf_op jit(solution)/shard_map/dot_general | solution.py:21
  338.6 14.5 %all-reduce.15 = bf16[640,128]{1,0:T(8,128)(2,1)} all-reduce(f32[640,128]{1,0:T(8,128)S(1)} %convolution_bitcast_fusion.3), channel_id=1, replica_groups=mesh['subj'=8,'vox'=4] {'vox'}, use_global_device_ids=true, to_apply=%region_7.10 | all-reduce | flops 81920 | bytes 491520 | tf_op jit(solution)/shard_map/psum | solution.py:22
  353.1 11.1 %convolution_bitcast_fusion = f32[12288,128]{0,1:T(8,128)} fusion(bf16[640,12288]{1,0:T(8,128)(2,1)} %param.7, bf16[640,128]{1,0:T(8,128)(2,1)} %all-reduce.15, pred[640]{0:T(1024)(128)(4,1)S(1)} %iota_compare_fusion.2), kind=kOutput, calls=%fused_computation | convolution fusion | flops 2013347840 | bytes 22184576 | tf_op jit(solution)/shard_map/dot_general | solution.py:25
  364.5 211.2 %all-reduce.11.cloned.1.call-done = f32[12288,128]{0,1:T(8,128)} async-done(((f32[12288,128]{0,1:T(8,128)}), f32[12288,128]{0,1:T(8,128)}) %all-reduce.11.cloned.1.call-update) | async-done | bytes 6291472 | tf_op jit(solution)/shard_map/psum | solution.py:24
  575.7 8.8 %fusion.20 = f32[128,128]{0,1:T(8,128)} fusion(f32[12288,128]{0,1:T(8,128)} %all-reduce.11.cloned.1.call-done), kind=kOutput, calls=%fused_computation.41 | convolution fusion | flops 2415919104 | bytes 6356992 | tf_op jit(solution)/shard_map/dot_general | solution.py:30
  584.6 30.2 %all-reduce.13.cloned.1.call-done = f32[128,128]{0,1:T(8,128)} async-done(((f32[128,128]{0,1:T(8,128)}), f32[128,128]{0,1:T(8,128)}) %all-reduce.13.cloned.1.call-update) | async-done | bytes 65552 | tf_op jit(solution)/shard_map/psum | solution.py:31
  615.7 0.9 fusion.9
  616.6 11.7 %cholesky.55 = f32[128,128]{1,0:T(8,128)S(1)} custom-call(f32[128,128]{1,0:T(8,128)S(1)} %fusion.9), custom_call_target="Cholesky" | custom-call | tf_op jit(solution)/shard_map/jit(cholesky)/cholesky | solution.py:32
  629.6 9.8 %custom-call.7 = f32[1,128,128]{1,2,0:T(8,128)S(1)} custom-call(f32[1,128,128]{2,1,0:T(8,128)S(1)} %fusion.7), custom_call_target="InvertDiagBlocksLowerTriangular" | custom-call | tf_op jit(solution)/shard_map/jit(_solve_triangular)/triangular_solve | solution.py:33
  639.5 9.2 %convolution_bitcast_fusion.2 = f32[12288,128]{0,1:T(8,128)} fusion(f32[12288,128]{0,1:T(8,128)} %all-reduce.11.cloned.1.call-done, f32[1,128,128]{1,2,0:T(8,128)S(1)} %custom-call.7), kind=kOutput, calls=%fused_computation.2 | convolution fusion | flops 2415919104 | bytes 12648448 | tf_op jit(solution)/shard_map/jit(_solve_triangular)/triangular_solve | solution.py:33
  648.7 6.6 copy.9
  (20 shorter events, 5.0 us)
Async XLA Ops:
  6.5 4.2 copy-start
  6.5 253.1 %all-reduce.7.cloned.1.call-start = ((), (), s32[]{:S(2)}) async-start(), calls=%async_computation | async-start | bytes 12582912 | tf_op jit(solution)/shard_map/psum | solution.py:24
  47.2 251.5 %all-reduce.9.cloned.1.call-start = ((), (), s32[]{:S(2)}) async-start(), calls=%async_computation.1 | async-start | bytes 131072 | tf_op jit(solution)/shard_map/psum | solution.py:31
  268.5 307.3 %all-reduce.11.cloned.1.call-start = ((), (), s32[]{:S(2)}) async-start(), calls=%async_computation.2 | async-start | bytes 12582912 | tf_op jit(solution)/shard_map/psum | solution.py:24
  364.2 250.6 %all-reduce.13.cloned.1.call-start = ((), (), s32[]{:S(2)}) async-start(), calls=%async_computation.3 | async-start | bytes 131072 | tf_op jit(solution)/shard_map/psum | solution.py:31
Sparse Core Ops, SparseCore 0:
  47.3 212.2 all-reduce.6
  268.6 30.0 all-reduce.8
  364.3 211.3 all-reduce.10
  584.7 30.0 all-reduce.12
where the time goes:
time: 662 us
  waiting for transfers between devices  484 us (73%)
  matrix products  72.6 us (11%)
  other arithmetic  53.3 us (8%)
  blocking collectives  31.6 us (5%)
  between operations  13.2 us (2%)
  local copies, waits for them, and re-layouts  6.73 us (1%)
    psum x2, waiting for transfers between devices, on_device(): lax.psum(lax.dot_general(scans, scores, (((0,), (0,)), ((), ())), preferr...  424 us
    psum x2, waiting for transfers between devices, on_device(): gram_matrix = lax.psum(local_gram, 'vox') / V  60.2 us
    psum x2, blocking collectives, on_device(): summed = lax.psum(partial_scores, 'vox')  31.6 us
    another operation x6, other arithmetic, on_device(): factor = jnp.linalg.cholesky(gram_matrix)  24.8 us
    dot_general x2, matrix products, on_device(): lax.dot_general(scans, scores, (((0,), (0,)), ((), ())), preferred_elemen...  22 us
    another operation x4, other arithmetic, on_device(): jax.scipy.linalg.solve_triangular(factor, sketch.T, lower=True)  20.9 us
    dot_general x2, matrix products, on_device(): local_gram = jnp.dot(sketch.T, sketch, precision=lax.Precision.HIGHEST)  17.6 us
    another operation x2, matrix products, on_device(): jax.scipy.linalg.solve_triangular(factor, sketch.T, lower=True)  16.8 us
  transfers between devices with their start and end apart: 4, of which 4 were waited for; matrix products, arithmetic and copies ran while one was open for 0% of the time, Pallas kernels for 0%

commit v1 on v0

v1 whole, which is shorter than its diff:
```python
import jax
import jax.numpy as jnp
from jax import lax
from jax.sharding import PartitionSpec as P

F32 = jnp.float32
BF16 = jnp.bfloat16
I16 = jnp.int16
HIGHEST = lax.Precision.HIGHEST
SCALE_ROWS = 16
STEPS = 64.0


def exchange(value, axis, size, mask):
    return lax.ppermute(value, axis, [(i, i ^ mask) for i in range(size)])


def butterfly(value, axis, size):
    mask = 1
    while mask < size:
        value = value + exchange(value, axis, size, mask)
        mask *= 2
    return value


class Plain:
    pad = 0

    @staticmethod
    def encode(value):
        return value.astype(BF16)

    @staticmethod
    def decode(sent):
        return sent.astype(F32)


class Fixed:
    pad = SCALE_ROWS

    @staticmethod
    def encode(value):
        top = jnp.maximum(jnp.max(jnp.abs(value), axis=0, keepdims=True), 1e-30)
        power = jnp.ceil(jnp.log2(top * (1.0 / 32000.0)) * STEPS)
        codes = jnp.round(value * jnp.exp2(power * (-1.0 / STEPS)))
        codes = jnp.clip(codes, -32767.0, 32767.0)
        rows = jnp.broadcast_to(power, (SCALE_ROWS, value.shape[1]))
        return jnp.concatenate([codes, rows]).astype(jnp.int32).astype(I16)

    @staticmethod
    def decode(sent):
        wide = sent.astype(jnp.int32).astype(F32)
        power = wide[-SCALE_ROWS : -SCALE_ROWS + 1]
        return wide[:-SCALE_ROWS] * jnp.exp2(power * (1.0 / STEPS))


def pick(pieces, index):
    return lax.dynamic_index_in_dim(pieces, index, 0, keepdims=False)


def reduce_scatter(first, second, code, axis, size, low, high):
    me = lax.axis_index(axis)
    mine_low, mine_high = me % low, me // low
    n, cols = first.shape[2], first.shape[3]
    m = second.shape[2]
    sent = code.encode(pick(first, 1 - mine_low).reshape(high * n, cols))
    got_first = exchange(sent, axis, size, 1)
    got_second = []
    for k in range(1, high):
        sent = code.encode(pick(second, mine_high ^ k).reshape(low * m, cols))
        got_second.append(exchange(sent, axis, size, k * low))
    first = pick(first, mine_low) + code.decode(got_first).reshape(high, n, cols)
    got = []
    for k in range(1, high):
        got.append(exchange(code.encode(pick(first, mine_high ^ k)), axis, size, k * low))
    second = pick(second, mine_high).reshape(low * m, cols)
    for part in got_second:
        second = second + code.decode(part)
    second = second.reshape(low, m, cols)
    got_low = exchange(code.encode(pick(second, 1 - mine_low)), axis, size, 1)
    first = pick(first, mine_high)
    for part in got:
        first = first + code.decode(part)
    return first, pick(second, mine_low) + code.decode(got_low)


def place(own, others, mine, count):
    out = jnp.zeros((count,) + own.shape, own.dtype)
    out = lax.dynamic_update_index_in_dim(out, own, mine, 0)
    for k, part in others:
        out = lax.dynamic_update_index_in_dim(out, part, mine ^ k, 0)
    return out


def all_gather(first, second, axis, size, low, high):
    me = lax.axis_index(axis)
    mine_low, mine_high = me % low, me // low
    got_low = exchange(second, axis, size, 1)
    got = [(k, exchange(first, axis, size, k * low)) for k in range(1, high)]
    second = place(second, [(1, got_low)], mine_low, low)
    got_second = [(k, exchange(second, axis, size, k * low)) for k in range(1, high)]
    first = place(first, got, mine_high, high)
    got_first = exchange(first, axis, size, 1)
    second = place(second, got_second, mine_high, high)
    first = place(first, [(1, got_first)], mine_low, low)
    return first, second


def inverse_factor(gram):
    factor = jnp.linalg.cholesky(gram)
    eye = jnp.eye(gram.shape[0], dtype=F32)
    return jax.scipy.linalg.solve_triangular(factor, eye, lower=True)


def make(mesh):
    subjects, blocks = mesh.shape["subj"], mesh.shape["vox"]
    low = 2
    high = subjects // low

    def on_device(scans, test_matrix, lengths, block_subject):
        time_rows, voxels = scans.shape
        rank = test_matrix.shape[1]
        all_voxels = voxels * blocks
        position = lax.axis_index("subj")
        slot_ids = jnp.arange(block_subject.shape[0], dtype=jnp.int32)
        subject = jnp.sum(jnp.where(slot_ids == position, block_subject, 0))
        length = jnp.sum(jnp.where(slot_ids == subject, lengths, 0))
        live_rows = (jnp.arange(time_rows, dtype=jnp.int32) < length)[:, None]
        cut = voxels * 2 // 3

        def sketch_sum(scores, code):
            partial = lax.dot_general(
                scans, scores, (((0,), (0,)), ((), ())), preferred_element_type=F32
            )
            first = partial[:cut].reshape(low, high, cut // subjects, rank)
            second = partial[cut:].reshape(high, low, (voxels - cut) // subjects, rank)
            return reduce_scatter(first, second, code, "subj", subjects, low, high)

        def gather(first, second):
            return all_gather(first, second, "subj", subjects, low, high)

        partial = jnp.dot(scans, test_matrix, preferred_element_type=F32)
        summed = butterfly(partial, "vox", blocks)
        scores = jnp.where(live_rows, summed, 0.0).astype(BF16)

        first, second = sketch_sum(scores, Plain)
        first, second = gather(first.astype(BF16), second.astype(BF16))
        sketch = jnp.concatenate([first.reshape(-1, rank), second.reshape(-1, rank)])
        raw = jnp.dot(scans, sketch, preferred_element_type=F32)
        local = lax.dot_general(
            sketch, sketch, (((0,), (0,)), ((), ())), preferred_element_type=F32
        )
        both = butterfly(jnp.concatenate([raw, local]), "vox", blocks)
        inverse = inverse_factor(both[time_rows:] / all_voxels)
        scores = jnp.dot(both[:time_rows], inverse.T, precision=HIGHEST)
        scores = jnp.where(live_rows, scores, 0.0).astype(BF16)

        first, second = sketch_sum(scores, Fixed)
        whole = gather(Fixed.encode(first), Fixed.encode(second))
        own = jnp.concatenate([first, second])
        local = lax.dot_general(own, own, (((0,), (0,)), ((), ())), precision=HIGHEST)
        gram = butterfly(butterfly(local, "vox", blocks), "subj", subjects)
        inverse = inverse_factor(gram / all_voxels)
        parts = []
        for part in whole:
            part = part.reshape((subjects,) + part.shape[2:])
            parts.append(jax.vmap(Fixed.decode)(part).reshape(-1, rank))
        return jnp.dot(jnp.concatenate(parts), inverse.T, precision=HIGHEST)

    return on_device


def solution(mesh):
    placed = (P("subj", "vox"), P("vox", None), P(), P())
    return jax.shard_map(
        make(mesh), mesh=mesh, in_specs=placed, out_specs=P("vox", None), check_vma=False
    )
```

time: 662 us -> 407 us (0.61); the launches traced: 662 us -> 399 us
  waiting for transfers between devices: 484 us -> 153 us
  starting transfers between devices: 0.53 us -> 66 us
  local copies, waits for them, and re-layouts: 6.73 us -> 62.8 us
  blocking collectives: 31.6 us -> 0 us
  matrix products: 72.6 us -> 44.5 us
  other arithmetic: 53.3 us -> 71.9 us
  between operations: 13.2 us -> 1.21 us
    psum x4 -> x0, waiting for transfers between devices: 484 us -> none  [the longest x2 424 us: on_device(): lax.psum(lax.dot_general(scans, scores, (((0,), (0,)), ((), ())), preferr...]
    ppermute x0 -> x41, waiting for transfers between devices: none -> 153 us  [exchange(): return lax.ppermute(value, axis, [(i, i ^ mask) for i in range(size)])]
    ppermute x0 -> x41, starting transfers between devices: none -> 66 us  [exchange(): return lax.ppermute(value, axis, [(i, i ^ mask) for i in range(size)])]
    psum x2 -> x0, blocking collectives: 31.6 us -> none  [on_device(): summed = lax.psum(partial_scores, 'vox')]
    reshape x0 -> x4, local copies, waits for them, and re-layouts: none -> 17.8 us  [the longest x2 12 us: sketch_sum(): first = partial[:cut].reshape(low, high, cut // subjects, rank)]
    another operation x2, matrix products: 16.8 us -> 0.57 us  [inverse_factor(): return jax.scipy.linalg.solve_triangular(factor, eye, lower=True)]
    dot_general x6 -> x8, matrix products: 55.8 us -> 43.9 us  [the longest x2 14 us: sketch_sum(): lax.dot_general(scans, scores, (((0,), (0,)), ((), ())), preferred_elemen...]
    unnamed x2 -> x23, local copies, waits for them, and re-layouts: 0.01 us -> 11.7 us
  transfers between devices with their start and end apart: 4 -> 41, of which waited for: 4 -> 23; matrix products, arithmetic and copies ran while one was open for 0% -> 18% of each run, Pallas kernels for 0% -> 0%
where the time goes in v1:
time: 407 us; the launch traced here: 399 us
  waiting for transfers between devices  153 us (38%)
  other arithmetic  71.9 us (18%)
  starting transfers between devices  66 us (16%)
  local copies, waits for them, and re-layouts  62.8 us (15%)
  matrix products  44.5 us (11%)
    ppermute x41, waiting for transfers between devices, exchange(): return lax.ppermute(value, axis, [(i, i ^ mask) for i in range(size)])  153 us
    ppermute x41, starting transfers between devices, exchange(): return lax.ppermute(value, axis, [(i, i ^ mask) for i in range(size)])  66 us
    another operation x6, other arithmetic, inverse_factor(): factor = jnp.linalg.cholesky(gram)  24.7 us
    another operation x4, other arithmetic, inverse_factor(): return jax.scipy.linalg.solve_triangular(factor, eye, lower=True)  21.4 us
    dot_general x2, matrix products, sketch_sum(): lax.dot_general(scans, scores, (((0,), (0,)), ((), ())), preferred_elemen...  14 us
    reshape x2, local copies, waits for them, and re-layouts, sketch_sum(): first = partial[:cut].reshape(low, high, cut // subjects, rank)  12 us
    unnamed x23, local copies, waits for them, and re-layouts  11.7 us
    dot_general x1, matrix products, on_device(): raw = jnp.dot(scans, sketch, preferred_element_type=F32)  10.7 us
  transfers between devices with their start and end apart: 41, of which 23 were waited for; matrix products, arithmetic and copies ran while one was open for 18% of the time, Pallas kernels for 0%

profile of v1, /device:TPU:0, one launch (start us, length us, event | category | flops | bytes accessed | tf_op | source)
XLA Modules:
  0.0 399.1 jit_solution(3807792949985573073)
XLA Ops:
  1.9 7.7 %fusion.106 = f32[640,128]{1,0:T(8,128)S(1)} fusion(bf16[640,12288]{1,0:T(8,128)(2,1)} %param.7, bf16[12288,128]{1,0:T(8,128)(2,1)S(1)} %copy-done), kind=kOutput, calls=%fused_computation.248 | convolution fusion | flops 2013265920 | bytes 19202048 | tf_op jit(solution)/shard_map/dot_general | solution.py:142
  16.9 5.4 %collective-permute-done.1 = f32[640,128]{1,0:T(8,128)S(1)} collective-permute-done((f32[640,128]{1,0:T(8,128)S(1)}, f32[640,128]{1,0:T(8,128)S(1)}, u32[]{:S(2)}, u32[]{:S(2)}) %collective-permute-start.1) | collective-permute-done | bytes 327712 | tf_op jit(solution)/shard_map/ppermute | solution.py:15
  22.3 7.1 %convolution_bitcast_fusion.1 = f32[12288,128]{0,1:T(8,128)S(1)} fusion(bf16[640,12288]{1,0:T(8,128)(2,1)} %param.7, f32[640,128]{1,0:T(8,128)S(1)} %add.167, f32[640,128]{1,0:T(8,128)S(1)} %collective-permute-done.1, pred[640]{0:T(1024)(128)(4,1)S(1)} %iota_compare_fusion.4), kind=kOutput, calls=%fused_computation.1 | convolution fusion | flops 2013511680 | bytes 22676096 | tf_op jit(solution)/shard_map/dot_general | solution.py:132
  34.4 6.0 %reshape.357 = f32[2,4,1024,128]{2,1,0,3:T(4,128)} reshape(f32[8192,128]{0,1:T(8,128)} %slice.112) | data formatting | bytes 8388608 | tf_op jit(solution)/shard_map/reshape | solution.py:135
  65.8 12.7 %collective-permute-done.11 = bf16[1024,128]{1,0:T(8,128)(2,1)} collective-permute-done((bf16[1024,128]{1,0:T(8,128)(2,1)}, bf16[1024,128]{1,0:T(8,128)(2,1)}, u32[]{:S(2)}, u32[]{:S(2)}) %collective-permute-start.11) | collective-permute-done | bytes 262176 | tf_op jit(solution)/shard_map/ppermute | solution.py:15
  88.0 5.0 %collective-permute-done.5 = bf16[1024,128]{1,0:T(8,128)(2,1)S(1)} collective-permute-done((bf16[1024,128]{1,0:T(8,128)(2,1)S(1)}, bf16[1024,128]{1,0:T(8,128)(2,1)S(1)}, u32[]{:S(2)}, u32[]{:S(2)}) %collective-permute-start.5) | collective-permute-done | bytes 262176 | tf_op jit(solution)/shard_map/ppermute | solution.py:15
  93.0 11.2 %collective-permute-done.4 = bf16[1024,128]{1,0:T(8,128)(2,1)S(1)} collective-permute-done((bf16[1024,128]{1,0:T(8,128)(2,1)S(1)}, bf16[1024,128]{1,0:T(8,128)(2,1)S(1)}, u32[]{:S(2)}, u32[]{:S(2)}) %collective-permute-start.4) | collective-permute-done | bytes 262176 | tf_op jit(solution)/shard_map/ppermute | solution.py:15
  111.6 7.9 %collective-permute-done.6 = bf16[1024,128]{1,0:T(8,128)(2,1)S(1)} collective-permute-done((bf16[1024,128]{1,0:T(8,128)(2,1)S(1)}, bf16[1024,128]{1,0:T(8,128)(2,1)S(1)}, u32[]{:S(2)}, u32[]{:S(2)}) %collective-permute-start.6) | collective-permute-done | bytes 262176 | tf_op jit(solution)/shard_map/ppermute | solution.py:15
  121.6 17.4 %collective-permute-done.8 = bf16[1024,128]{1,0:T(8,128)(2,1)S(1)} collective-permute-done((bf16[1024,128]{1,0:T(8,128)(2,1)S(1)}, bf16[1024,128]{1,0:T(8,128)(2,1)S(1)}, u32[]{:S(2)}, u32[]{:S(2)}) %collective-permute-start.8) | collective-permute-done | bytes 262176 | tf_op jit(solution)/shard_map/ppermute | solution.py:15
  142.9 18.5 %collective-permute-done.9 = bf16[4,1024,128]{2,1,0:T(8,128)(2,1)S(1)} collective-permute-done((bf16[4,1024,128]{2,1,0:T(8,128)(2,1)S(1)}, bf16[4,1024,128]{2,1,0:T(8,128)(2,1)S(1)}, u32[]{:S(2)}, u32[]{:S(2)}) %collective-permute-start.9) | collective-permute-done | bytes 1048608 | tf_op jit(solution)/shard_map/ppermute | solution.py:15
  162.7 10.7 %fusion.9 = f32[640,128]{0,1:T(8,128)S(1)} fusion(bf16[640,12288]{1,0:T(8,128)(2,1)} %param.7, bf16[4096,128]{1,0:T(8,128)(2,1)} %bitcast.236, bf16[8192,128]{1,0:T(8,128)(2,1)S(1)} %bitcast.232), kind=kOutput, calls=%fused_computation.25 | convolution fusion | flops 2019557376 | bytes 19202048 | tf_op jit(solution)/shard_map/dot_general | solution.py:149
  176.9 9.6 %collective-permute-done.19 = f32[768,128]{0,1:T(8,128)S(1)} collective-permute-done((f32[768,128]{0,1:T(8,128)S(1)}, f32[768,128]{0,1:T(8,128)S(1)}, u32[]{:S(2)}, u32[]{:S(2)}) %collective-permute-start.19) | collective-permute-done | bytes 393248 | tf_op jit(solution)/shard_map/ppermute | solution.py:15
  186.6 11.7 %cholesky.44 = f32[128,128]{1,0:T(8,128)S(1)} custom-call(f32[128,128]{1,0:T(8,128)S(1)} %fusion.75), custom_call_target="Cholesky" | custom-call | tf_op jit(solution)/shard_map/jit(cholesky)/cholesky | solution.py:110
  199.7 10.2 %custom-call.6 = f32[1,128,128]{1,2,0:T(8,128)S(1)} custom-call(f32[1,128,128]{2,1,0:T(8,128)S(1)} %fusion.70), custom_call_target="InvertDiagBlocksLowerTriangular" | custom-call | tf_op jit(solution)/shard_map/jit(_solve_triangular)/triangular_solve | solution.py:112
  210.9 7.0 %convolution_bitcast_fusion = f32[12288,128]{0,1:T(8,128)S(1)} fusion(bf16[640,128]{1,0:T(8,128)(2,1)S(1)} %fusion.10, bf16[640,12288]{1,0:T(8,128)(2,1)} %param.7), kind=kOutput, calls=%fused_computation | convolution fusion | flops 2013265920 | bytes 22183936 | tf_op jit(solution)/shard_map/dot_general | solution.py:132
  231.8 12.5 %collective-permute-start.29 = (s16[1040,128]{1,0:T(8,128)(2,1)}, s16[1040,128]{1,0:T(8,128)(2,1)}, u32[]{:S(2)}, u32[]{:S(2)}) collective-permute-start(s16[1040,128]{1,0:T(8,128)(2,1)} %fusion.21), channel_id=1, source_target_pairs={{0,16},{4,20},{8,24},{12,28},{16,0},{20,4},{24,8},{28,12},{1,17},{... | collective-permute-start | bytes 798728 | tf_op jit(solution)/shard_map/ppermute | solution.py:15
  245.4 6.0 %reshape.365 = f32[2,4,1024,128]{2,1,0,3:T(4,128)} reshape(f32[8192,128]{0,1:T(8,128)} %slice.116) | data formatting | bytes 8388608 | tf_op jit(solution)/shard_map/reshape | solution.py:135
  282.6 16.2 %collective-permute-done.34 = s16[2,528,128]{2,1,0:T(8,128)(2,1)S(1)} collective-permute-done((s16[2,528,128]{2,1,0:T(8,128)(2,1)S(1)}, s16[2,528,128]{2,1,0:T(8,128)(2,1)S(1)}, u32[]{:S(2)}, u32[]{:S(2)}) %collective-permute-start.34) | collective-permute-done | bytes 270368 | tf_op jit(solution)/shard_map/ppermute | solution.py:15
  309.8 5.7 %collective-permute-done.23 = s16[1040,128]{1,0:T(8,128)(2,1)S(1)} collective-permute-done((s16[1040,128]{1,0:T(8,128)(2,1)S(1)}, s16[1040,128]{1,0:T(8,128)(2,1)S(1)}, u32[]{:S(2)}, u32[]{:S(2)}) %collective-permute-start.23) | collective-permute-done | bytes 266272 | tf_op jit(solution)/shard_map/ppermute | solution.py:15
  315.6 11.9 %collective-permute-done.22 = s16[1040,128]{1,0:T(8,128)(2,1)S(1)} collective-permute-done((s16[1040,128]{1,0:T(8,128)(2,1)S(1)}, s16[1040,128]{1,0:T(8,128)(2,1)S(1)}, u32[]{:S(2)}, u32[]{:S(2)}) %collective-permute-start.22) | collective-permute-done | bytes 266272 | tf_op jit(solution)/shard_map/ppermute | solution.py:15
  341.3 9.9 %collective-permute-done.39 = f32[128,128]{0,1:T(8,128)S(1)} collective-permute-done((f32[128,128]{0,1:T(8,128)S(1)}, f32[128,128]{0,1:T(8,128)S(1)}, u32[]{:S(2)}, u32[]{:S(2)}) %collective-permute-start.39) | collective-permute-done | bytes 65568 | tf_op jit(solution)/shard_map/ppermute | solution.py:15
  363.8 11.7 %cholesky.55 = f32[128,128]{1,0:T(8,128)S(1)} custom-call(f32[128,128]{1,0:T(8,128)S(1)} %fusion.73), custom_call_target="Cholesky" | custom-call | tf_op jit(solution)/shard_map/jit(cholesky)/cholesky | solution.py:110
  376.7 10.0 %custom-call.7 = f32[1,128,128]{1,2,0:T(8,128)S(1)} custom-call(f32[1,128,128]{2,1,0:T(8,128)S(1)} %fusion.71), custom_call_target="InvertDiagBlocksLowerTriangular" | custom-call | tf_op jit(solution)/shard_map/jit(_solve_triangular)/triangular_solve | solution.py:112
  390.6 8.3 %fusion = f32[12288,128]{1,0:T(8,128)} fusion(f32[128,128]{1,0:T(8,128)S(1)} %fusion.66, f32[4096,128]{1,0:T(8,128)S(1)} %bitcast.227, f32[8192,128]{1,0:T(8,128)S(1)} %bitcast.223), kind=kOutput, calls=%fused_computation.2 | convolution fusion | flops 2417491968 | bytes 12648448 | tf_op jit(solution)/shard_map/dot_general | solution.py:168
  (247 shorter events, 157.6 us)
Async XLA Ops:
  44.2 36.1 %collective-permute-start.2 = (bf16[4096,128]{1,0:T(8,128)(2,1)}, bf16[4096,128]{1,0:T(8,128)(2,1)}, u32[]{:S(2)}, u32[]{:S(2)}) collective-permute-start(bf16[4096,128]{1,0:T(8,128)(2,1)} %bitcast.2), channel_id=1, source_target_pairs={{0,4},{4,0},{8,12},{12,8},{16,20},{20,16},{24,28},{28,24},{1,5},{5... | collective-permute-start | bytes 3145736 | tf_op jit(solution)/shard_map/ppermute | solution.py:15
  57.6 20.9 %collective-permute-start.11 = (bf16[1024,128]{1,0:T(8,128)(2,1)}, bf16[1024,128]{1,0:T(8,128)(2,1)}, u32[]{:S(2)}, u32[]{:S(2)}) collective-permute-start(bf16[1024,128]{1,0:T(8,128)(2,1)} %bitcast.17), channel_id=1, source_target_pairs={{0,16},{4,20},{8,24},{12,28},{16,0},{20,4},{24,8},{28,12},{1,17},{... | collective-permute-start | bytes 786440 | tf_op jit(solution)/shard_map/ppermute | solution.py:15
  58.5 20.0 %collective-permute-start.10 = (bf16[1024,128]{1,0:T(8,128)(2,1)}, bf16[1024,128]{1,0:T(8,128)(2,1)}, u32[]{:S(2)}, u32[]{:S(2)}) collective-permute-start(bf16[1024,128]{1,0:T(8,128)(2,1)} %bitcast.16), channel_id=1, source_target_pairs={{0,8},{4,12},{8,0},{12,4},{16,24},{20,28},{24,16},{28,20},{1,9},{5... | collective-permute-start | bytes 786440 | tf_op jit(solution)/shard_map/ppermute | solution.py:15
  84.4 19.9 %collective-permute-start.4 = (bf16[1024,128]{1,0:T(8,128)(2,1)S(1)}, bf16[1024,128]{1,0:T(8,128)(2,1)S(1)}, u32[]{:S(2)}, u32[]{:S(2)}) collective-permute-start(bf16[1024,128]{1,0:T(8,128)(2,1)S(1)} %get-tuple-element.58), channel_id=1, source_target_pairs={{0,16},{4,20},{8,24},{12,28},{16,0},{20,4},{24,8},{28,12},{1,17},{... | collective-permute-start | bytes 786440 | tf_op jit(solution)/shard_map/ppermute | solution.py:15
  84.4 19.9 %collective-permute-start.3 = (bf16[1024,128]{1,0:T(8,128)(2,1)S(1)}, bf16[1024,128]{1,0:T(8,128)(2,1)S(1)}, u32[]{:S(2)}, u32[]{:S(2)}) collective-permute-start(bf16[1024,128]{1,0:T(8,128)(2,1)S(1)} %get-tuple-element.56), channel_id=1, source_target_pairs={{0,8},{4,12},{8,0},{12,4},{16,24},{20,28},{24,16},{28,20},{1,9},{5... | collective-permute-start | bytes 786440 | tf_op jit(solution)/shard_map/ppermute | solution.py:15
  86.4 20.8 %collective-permute-start.14 = (bf16[512,128]{1,0:T(8,128)(2,1)S(1)}, bf16[512,128]{1,0:T(8,128)(2,1)S(1)}, u32[]{:S(2)}, u32[]{:S(2)}) collective-permute-start(bf16[512,128]{1,0:T(8,128)(2,1)S(1)} %get-tuple-element.45), channel_id=1, source_target_pairs={{0,4},{4,0},{8,12},{12,8},{16,20},{20,16},{24,28},{28,24},{1,5},{5... | collective-permute-start | bytes 393224 | tf_op jit(solution)/shard_map/ppermute | solution.py:15
  104.7 16.9 %collective-permute-start.7 = (bf16[1024,128]{1,0:T(8,128)(2,1)S(1)}, bf16[1024,128]{1,0:T(8,128)(2,1)S(1)}, u32[]{:S(2)}, u32[]{:S(2)}) collective-permute-start(bf16[1024,128]{1,0:T(8,128)(2,1)S(1)} %get-tuple-element.43), channel_id=1, source_target_pairs={{0,16},{4,20},{8,24},{12,28},{16,0},{20,4},{24,8},{28,12},{1,17},{... | collective-permute-start | bytes 786440 | tf_op jit(solution)/shard_map/ppermute | solution.py:15
  107.2 33.7 %collective-permute-start.15 = (bf16[2,512,128]{2,1,0:T(8,128)(2,1)S(1)}, bf16[2,512,128]{2,1,0:T(8,128)(2,1)S(1)}, u32[]{:S(2)}, u32[]{:S(2)}) collective-permute-start(bf16[2,512,128]{2,1,0:T(8,128)(2,1)S(1)} %bitcast_dynamic-update-slice_fusion.20), channel_id=1, source_target_pairs={{0,8},{4,12},{8,0},{12,4},{16,24},{20,28},{24,16},{28,20},{1,9},{5... | collective-permute-start | bytes 786440 | tf_op jit(solution)/shard_map/ppermute | solution.py:15
  107.3 35.1 %collective-permute-start.16 = (bf16[2,512,128]{2,1,0:T(8,128)(2,1)S(1)}, bf16[2,512,128]{2,1,0:T(8,128)(2,1)S(1)}, u32[]{:S(2)}, u32[]{:S(2)}) collective-permute-start(bf16[2,512,128]{2,1,0:T(8,128)(2,1)S(1)} %bitcast_dynamic-update-slice_fusion.20), channel_id=1, source_target_pairs={{0,16},{4,20},{8,24},{12,28},{16,0},{20,4},{24,8},{28,12},{1,17},{... | collective-permute-start | bytes 786440 | tf_op jit(solution)/shard_map/ppermute | solution.py:15
  109.7 32.8 %collective-permute-start.17 = (bf16[2,512,128]{2,1,0:T(8,128)(2,1)S(1)}, bf16[2,512,128]{2,1,0:T(8,128)(2,1)S(1)}, u32[]{:S(2)}, u32[]{:S(2)}) collective-permute-start(bf16[2,512,128]{2,1,0:T(8,128)(2,1)S(1)} %bitcast_dynamic-update-slice_fusion.20), channel_id=1, source_target_pairs={{0,24},{4,28},{8,16},{12,20},{16,8},{20,12},{24,0},{28,4},{1,25},{... | collective-permute-start | bytes 786440 | tf_op jit(solution)/shard_map/ppermute | solution.py:15
  119.5 19.5 %collective-permute-start.8 = (bf16[1024,128]{1,0:T(8,128)(2,1)S(1)}, bf16[1024,128]{1,0:T(8,128)(2,1)S(1)}, u32[]{:S(2)}, u32[]{:S(2)}) collective-permute-start(bf16[1024,128]{1,0:T(8,128)(2,1)S(1)} %get-tuple-element.43), channel_id=1, source_target_pairs={{0,24},{4,28},{8,16},{12,20},{16,8},{20,12},{24,0},{28,4},{1,25},{... | collective-permute-start | bytes 786440 | tf_op jit(solution)/shard_map/ppermute | solution.py:15
  139.1 22.4 %collective-permute-start.9 = (bf16[4,1024,128]{2,1,0:T(8,128)(2,1)S(1)}, bf16[4,1024,128]{2,1,0:T(8,128)(2,1)S(1)}, u32[]{:S(2)}, u32[]{:S(2)}) collective-permute-start(bf16[4,1024,128]{2,1,0:T(8,128)(2,1)S(1)} %bitcast_dynamic-update-slice_fusion.15), channel_id=1, source_target_pairs={{0,4},{4,0},{8,12},{12,8},{16,20},{20,16},{24,28},{28,24},{1,5},{5... | collective-permute-start | bytes 3145736 | tf_op jit(solution)/shard_map/ppermute | solution.py:15
  228.7 30.3 %collective-permute-start.30 = (s16[1040,128]{1,0:T(8,128)(2,1)S(1)}, s16[1040,128]{1,0:T(8,128)(2,1)}, u32[]{:S(2)}, u32[]{:S(2)}) collective-permute-start(s16[1040,128]{1,0:T(8,128)(2,1)S(1)} %fusion.22), channel_id=1, source_target_pairs={{0,24},{4,28},{8,16},{12,20},{16,8},{20,12},{24,0},{28,4},{1,25},{... | collective-permute-start | bytes 798728 | tf_op jit(solution)/shard_map/ppermute | solution.py:15
  231.8 28.5 %collective-permute-start.29 = (s16[1040,128]{1,0:T(8,128)(2,1)}, s16[1040,128]{1,0:T(8,128)(2,1)}, u32[]{:S(2)}, u32[]{:S(2)}) collective-permute-start(s16[1040,128]{1,0:T(8,128)(2,1)} %fusion.21), channel_id=1, source_target_pairs={{0,16},{4,20},{8,24},{12,28},{16,0},{20,4},{24,8},{28,12},{1,17},{... | collective-permute-start | bytes 798728 | tf_op jit(solution)/shard_map/ppermute | solution.py:15
  245.4 16.0 %collective-permute-start.28 = (s16[1040,128]{1,0:T(8,128)(2,1)}, s16[1040,128]{1,0:T(8,128)(2,1)}, u32[]{:S(2)}, u32[]{:S(2)}) collective-permute-start(s16[1040,128]{1,0:T(8,128)(2,1)} %fusion.20), channel_id=1, source_target_pairs={{0,8},{4,12},{8,0},{12,4},{16,24},{20,28},{24,16},{28,20},{1,9},{5... | collective-permute-start | bytes 798728 | tf_op jit(solution)/shard_map/ppermute | solution.py:15
  276.2 24.6 %collective-permute-start.20 = (s16[4112,128]{1,0:T(8,128)(2,1)}, s16[4112,128]{1,0:T(8,128)(2,1)}, u32[]{:S(2)}, u32[]{:S(2)}) collective-permute-start(s16[4112,128]{1,0:T(8,128)(2,1)} %fusion.4), channel_id=1, source_target_pairs={{0,4},{4,0},{8,12},{12,8},{16,20},{20,16},{24,28},{28,24},{1,5},{5... | collective-permute-start | bytes 3158024 | tf_op jit(solution)/shard_map/ppermute | solution.py:15
  279.7 19.1 %collective-permute-start.34 = (s16[2,528,128]{2,1,0:T(8,128)(2,1)S(1)}, s16[2,528,128]{2,1,0:T(8,128)(2,1)S(1)}, u32[]{:S(2)}, u32[]{:S(2)}) collective-permute-start(s16[2,528,128]{2,1,0:T(8,128)(2,1)S(1)} %bitcast_dynamic-update-slice_fusion.19), channel_id=1, source_target_pairs={{0,16},{4,20},{8,24},{12,28},{16,0},{20,4},{24,8},{28,12},{1,17},{... | collective-permute-start | bytes 811016 | tf_op jit(solution)/shard_map/ppermute | solution.py:15
  280.5 18.4 %collective-permute-start.35 = (s16[2,528,128]{2,1,0:T(8,128)(2,1)S(1)}, s16[2,528,128]{2,1,0:T(8,128)(2,1)S(1)}, u32[]{:S(2)}, u32[]{:S(2)}) collective-permute-start(s16[2,528,128]{2,1,0:T(8,128)(2,1)S(1)} %bitcast_dynamic-update-slice_fusion.19), channel_id=1, source_target_pairs={{0,24},{4,28},{8,16},{12,20},{16,8},{20,12},{24,0},{28,4},{1,25},{... | collective-permute-start | bytes 811016 | tf_op jit(solution)/shard_map/ppermute | solution.py:15
  306.5 21.0 %collective-permute-start.22 = (s16[1040,128]{1,0:T(8,128)(2,1)S(1)}, s16[1040,128]{1,0:T(8,128)(2,1)S(1)}, u32[]{:S(2)}, u32[]{:S(2)}) collective-permute-start(s16[1040,128]{1,0:T(8,128)(2,1)S(1)} %fusion.16), channel_id=1, source_target_pairs={{0,16},{4,20},{8,24},{12,28},{16,0},{20,4},{24,8},{28,12},{1,17},{... | collective-permute-start | bytes 798728 | tf_op jit(solution)/shard_map/ppermute | solution.py:15
  309.7 17.9 %collective-permute-start.21 = (s16[1040,128]{1,0:T(8,128)(2,1)S(1)}, s16[1040,128]{1,0:T(8,128)(2,1)S(1)}, u32[]{:S(2)}, u32[]{:S(2)}) collective-permute-start(s16[1040,128]{1,0:T(8,128)(2,1)S(1)} %fusion.15), channel_id=1, source_target_pairs={{0,8},{4,12},{8,0},{12,4},{16,24},{20,28},{24,16},{28,20},{1,9},{5... | collective-permute-start | bytes 798728 | tf_op jit(solution)/shard_map/ppermute | solution.py:15
  332.3 22.0 %collective-permute-start.24 = (s16[1040,128]{1,0:T(8,128)(2,1)S(1)}, s16[1040,128]{1,0:T(8,128)(2,1)S(1)}, u32[]{:S(2)}, u32[]{:S(2)}) collective-permute-start(s16[1040,128]{1,0:T(8,128)(2,1)S(1)} %fusion.19), channel_id=1, source_target_pairs={{0,8},{4,12},{8,0},{12,4},{16,24},{20,28},{24,16},{28,20},{1,9},{5... | collective-permute-start | bytes 798728 | tf_op jit(solution)/shard_map/ppermute | solution.py:15
  335.7 23.0 %collective-permute-start.25 = (s16[1040,128]{1,0:T(8,128)(2,1)S(1)}, s16[1040,128]{1,0:T(8,128)(2,1)S(1)}, u32[]{:S(2)}, u32[]{:S(2)}) collective-permute-start(s16[1040,128]{1,0:T(8,128)(2,1)S(1)} %fusion.19), channel_id=1, source_target_pairs={{0,16},{4,20},{8,24},{12,28},{16,0},{20,4},{24,8},{28,12},{1,17},{... | collective-permute-start | bytes 798728 | tf_op jit(solution)/shard_map/ppermute | solution.py:15
  335.8 23.6 %collective-permute-start.26 = (s16[1040,128]{1,0:T(8,128)(2,1)S(1)}, s16[1040,128]{1,0:T(8,128)(2,1)S(1)}, u32[]{:S(2)}, u32[]{:S(2)}) collective-permute-start(s16[1040,128]{1,0:T(8,128)(2,1)S(1)} %fusion.19), channel_id=1, source_target_pairs={{0,24},{4,28},{8,16},{12,20},{16,8},{20,12},{24,0},{28,4},{1,25},{... | collective-permute-start | bytes 798728 | tf_op jit(solution)/shard_map/ppermute | solution.py:15
  360.1 26.9 %collective-permute-start.27 = (s16[4,1040,128]{2,1,0:T(8,128)(2,1)}, s16[4,1040,128]{2,1,0:T(8,128)(2,1)}, u32[]{:S(2)}, u32[]{:S(2)}) collective-permute-start(s16[4,1040,128]{2,1,0:T(8,128)(2,1)} %bitcast_dynamic-update-slice_fusion.8), channel_id=1, source_target_pairs={{0,4},{4,0},{8,12},{12,8},{16,20},{20,16},{24,28},{28,24},{1,5},{5... | collective-permute-start | bytes 3194888 | tf_op jit(solution)/shard_map/ppermute | solution.py:15
  (28 other events, 205.8 us)
